TPU v7x, 512 devices: a whole 4x8x8 slice. The times are simulated.
512 devices in a mesh: dp: 32 (over x, z_lo, core), seq: 16 (over y, z_hi).
Axes of the slice: x: 4, y: 8, z: 8 (z_hi: 2, z_lo: 4; z = z_hi * 4 + z_lo), core: 2. Of those that a mesh axis runs over, the one named last changes fastest.
Arguments:
- queries: bfloat16 [32, 2048, 512], P('dp', 'seq'), may hold values from -6 to 6
- keys: bfloat16 [32, 2048, 512], P('dp', 'seq'), may hold values from -6 to 6
- values: bfloat16 [32, 2048, 512], P('dp', 'seq'), may hold values from -30 to 30
- gates: bfloat16 [32, 2048, 512], P('dp', 'seq'), may hold values from -6 to 6
- d_out: bfloat16 [32, 2048, 1024], P('dp', 'seq'), may hold values from -6 to 6
- w_out: bfloat16 [512, 1024], replicated, may hold values from -0.25 to 0.25
- lengths: int32 [32, 4], P('dp'), may hold values from 1 to 1024, 2048 in all within a row
- tile_owner: int32 [32, 16], P('dp'), may hold values from 0 to 15, each once within a row
- pattern: int32 [32, 16, 16], P('dp'), may hold values 0 or 1
Outputs:
- layer_out: bfloat16 [32, 2048, 1024], P('dp', 'seq')
- query_grad: bfloat16 [32, 2048, 512], P('dp', 'seq')
- key_grad: bfloat16 [32, 2048, 512], P('dp', 'seq')
- value_grad: bfloat16 [32, 2048, 512], P('dp', 'seq')
- gate_grad: bfloat16 [32, 2048, 512], P('dp', 'seq')
- weight_grad: float32 [512, 1024], P('dp')
Inputs may be any that keep to these rules, and one draw needn't show every extreme that they name: Each group's lengths sum to 2048. `tile_owner`: each group's row is a permutation.
All inputs are finite; a program needn't handle non-finite values. No bound on the sum of `pattern` on one device may be relied on, other than what follows from the above.
Results may differ from a plain program's by a relative error of at most 0.0059.
Values may be sent and summed in bfloat16 or wider, within the bound.
A program may use at most 64 MiB of HBM per device.

v0:
```python
import jax
import jax.numpy as jnp
from jax import lax
from jax.sharding import PartitionSpec as P

H = 4
DH = 128


eps = 1e-06


def positions(row_index, owner_row, tile_rows):
    slot_ids = jnp.arange(owner_row.shape[0], dtype=jnp.int32)
    inverse = jnp.sum(
        jnp.where(owner_row[:, None] == slot_ids[None, :], slot_ids[:, None], 0),
        axis=0,
        dtype=jnp.int32,
    )
    device_of = row_index // tile_rows
    tile_of = jnp.sum(
        jnp.where(device_of[:, None] == slot_ids[None, :], inverse[None, :], 0),
        axis=1,
        dtype=jnp.int32,
    )
    return (tile_of, tile_of * tile_rows + row_index % tile_rows)


def users_of(position, user_lengths):
    user_ends = jnp.cumsum(user_lengths, dtype=jnp.int32)
    return jnp.sum(
        (position[:, None] >= user_ends[None, :]).astype(jnp.int32), axis=1, dtype=jnp.int32
    )


def describe(row_index, owner_row, user_lengths, tile_rows):
    tile_of, position = positions(row_index, owner_row, tile_rows)
    return (tile_of, position, users_of(position, user_lengths))


def block_mask(query_side, key_side, link_table):
    query_tiles, query_pos, query_users = query_side
    key_tiles, key_pos, key_users = key_side
    slot_ids = jnp.arange(link_table.shape[0], dtype=jnp.int32)
    query_hot = (query_tiles[:, None] == slot_ids[None, :]).astype(link_table.dtype)
    key_hot = (key_tiles[:, None] == slot_ids[None, :]).astype(link_table.dtype)
    linked = jnp.dot(jnp.dot(query_hot, link_table), key_hot.T)
    keep = (query_users[:, None] == key_users[None, :]) & (key_pos[None, :] <= query_pos[:, None])
    keep = keep & ((query_tiles[:, None] == key_tiles[None, :]) | (linked > 0.5))
    return keep.astype(jnp.float32)


def silu_slope(scores):
    sig_scores = jax.nn.sigmoid(scores)
    return sig_scores * (1.0 + scores * (1.0 - sig_scores))


def body(queries, keys, values, gates, d_out, w_out, lengths, tile_owner, pattern):
    query_rows = queries[0]
    key_rows = keys[0]
    value_rows = values[0]
    gate_rows = gates[0]
    out_grad = d_out[0]
    user_lengths = lengths[0]
    owner_row = tile_owner[0]
    link_table = pattern[0].astype(jnp.float32)
    tile_rows = query_rows.shape[0]
    feat_width = query_rows.shape[1]
    score_scale = DH ** (-0.5)
    seat_index = lax.axis_index("seq")
    mine = describe(
        seat_index * tile_rows + jnp.arange(tile_rows, dtype=jnp.int32),
        owner_row,
        user_lengths,
        tile_rows,
    )

    def others(piece_rows):
        return describe(jnp.arange(piece_rows, dtype=jnp.int32), owner_row, user_lengths, tile_rows)

    query_heads = query_rows.reshape(tile_rows, H, DH)
    key_heads = key_rows.reshape(tile_rows, H, DH)
    value_heads = value_rows.reshape(tile_rows, H, DH)
    key_part = lax.all_gather(key_rows, "seq", axis=0, tiled=True)
    value_part = lax.all_gather(value_rows, "seq", axis=0, tiled=True)
    piece_rows = key_part.shape[0]
    keep_mask = block_mask(mine, others(piece_rows), link_table)
    scores = (
        jnp.einsum(
            "qhd,khd->hqk",
            query_heads,
            key_part.reshape(piece_rows, H, DH),
            preferred_element_type=jnp.float32,
        )
        * score_scale
    )
    weights = (jax.nn.silu(scores) * keep_mask).astype(jnp.bfloat16)
    attended = jnp.einsum(
        "hqk,khd->qhd",
        weights,
        value_part.reshape(piece_rows, H, DH),
        preferred_element_type=jnp.float32,
    )
    attended = attended.reshape(tile_rows, feat_width)
    row_mean = jnp.mean(attended, axis=1, keepdims=True)
    centred = attended - row_mean
    inv_std = lax.rsqrt(jnp.mean(centred * centred, axis=1, keepdims=True) + eps)
    normed = centred * inv_std
    gates_f = gate_rows.astype(jnp.float32)
    gated = (normed * gates_f).astype(jnp.bfloat16)
    layer_out = jnp.dot(gated, w_out, preferred_element_type=jnp.float32).astype(jnp.bfloat16)
    d_gated = lax.dot_general(
        out_grad, w_out, (((1,), (1,)), ((), ())), preferred_element_type=jnp.float32
    )
    weight_part = lax.dot_general(
        gated, out_grad, (((0,), (0,)), ((), ())), preferred_element_type=jnp.float32
    )
    gate_grad = (d_gated * normed).astype(jnp.bfloat16)
    d_normed = d_gated * gates_f
    d_center = d_normed - jnp.mean(d_normed, axis=1, keepdims=True)
    d_attended = (
        (d_center - normed * jnp.mean(d_normed * normed, axis=1, keepdims=True)) * inv_std
    ).astype(jnp.bfloat16)
    d_att_heads = d_attended.reshape(tile_rows, H, DH)
    peer_query = lax.all_gather(query_rows, "seq", axis=0, tiled=True)
    peer_grad = lax.all_gather(d_attended, "seq", axis=0, tiled=True)
    piece_rows = peer_query.shape[0]
    keep_mask = block_mask(others(piece_rows), mine, link_table)
    peer_heads = peer_query.reshape(piece_rows, H, DH)
    peer_grad_heads = peer_grad.reshape(piece_rows, H, DH)
    scores = (
        jnp.einsum("qhd,khd->hqk", peer_heads, key_heads, preferred_element_type=jnp.float32)
        * score_scale
    )
    weights = (jax.nn.silu(scores) * keep_mask).astype(jnp.bfloat16)
    d_weights = jnp.einsum(
        "qhd,khd->hqk", peer_grad_heads, value_heads, preferred_element_type=jnp.float32
    )
    d_scores = (d_weights * silu_slope(scores) * keep_mask * score_scale).astype(jnp.bfloat16)
    key_run = jnp.einsum("hqk,qhd->khd", d_scores, peer_heads, preferred_element_type=jnp.float32)
    value_run = jnp.einsum(
        "hqk,qhd->khd", weights, peer_grad_heads, preferred_element_type=jnp.float32
    )
    key_part = lax.all_gather(key_rows, "seq", axis=0, tiled=True)
    value_part = lax.all_gather(value_rows, "seq", axis=0, tiled=True)
    query_piece_rows = key_part.shape[0]
    query_keep_mask = block_mask(mine, others(query_piece_rows), link_table)
    key_part_heads = key_part.reshape(query_piece_rows, H, DH)
    scores = (
        jnp.einsum("qhd,khd->hqk", query_heads, key_part_heads, preferred_element_type=jnp.float32)
        * score_scale
    )
    d_weights = jnp.einsum(
        "qhd,khd->hqk",
        d_att_heads,
        value_part.reshape(query_piece_rows, H, DH),
        preferred_element_type=jnp.float32,
    )
    d_scores = (d_weights * silu_slope(scores) * query_keep_mask * score_scale).astype(jnp.bfloat16)
    query_grad = jnp.einsum(
        "hqk,khd->qhd", d_scores, key_part_heads, preferred_element_type=jnp.float32
    )
    group_sum = lax.psum(weight_part, "seq")
    weight_grad = lax.psum_scatter(group_sum, "dp", scatter_dimension=0, tiled=True)
    query_out = query_grad.reshape(tile_rows, feat_width).astype(jnp.bfloat16)
    key_out = key_run.reshape(tile_rows, feat_width).astype(jnp.bfloat16)
    value_out = value_run.reshape(tile_rows, feat_width).astype(jnp.bfloat16)
    return (
        layer_out[None],
        query_out[None],
        key_out[None],
        value_out[None],
        gate_grad[None],
        weight_grad,
    )


def solution(mesh):
    in_specs = (
        P("dp", "seq", None),
        P("dp", "seq", None),
        P("dp", "seq", None),
        P("dp", "seq", None),
        P("dp", "seq", None),
        P(),
        P("dp", None),
        P("dp", None),
        P("dp", None, None),
    )
    out_specs = (
        P("dp", "seq", None),
        P("dp", "seq", None),
        P("dp", "seq", None),
        P("dp", "seq", None),
        P("dp", "seq", None),
        P("dp", None),
    )
    return jax.shard_map(body, mesh=mesh, in_specs=in_specs, out_specs=out_specs, check_vma=False)
```

profile of v0, /device:TPU:6, one launch (start us, length us, event | category | flops | bytes accessed | tf_op | source)
XLA Modules:
  0.0 784.0 jit_solution(10740476029546388242)
XLA Ops:
  8.0 1.7 copy.39
  9.7 1.7 copy.48
  14.4 1.6 fusion.2
  16.0 106.3 %all-gather.12.cloned.1.call-done = bf16[1,2048,512]{2,1,0:T(8,128)(2,1)} async-done(((bf16[1,128,512]{2,1,0:T(8,128)(2,1)}), bf16[1,2048,512]{2,1,0:T(8,128)(2,1)}) %all-gather.12.cloned.1.call-update) | async-done | bytes 2097168 | tf_op jit(solution)/shard_map/all_gather | solution.py:85
  122.3 4.0 copy.42
  126.3 101.5 %all-gather.10.cloned.1.call-done = bf16[1,2048,512]{1,2,0:T(8,128)(2,1)} async-done(((bf16[1,128,512]{1,2,0:T(8,128)(2,1)}), bf16[1,2048,512]{1,2,0:T(8,128)(2,1)}) %all-gather.10.cloned.1.call-update) | async-done | bytes 2097168 | tf_op jit(solution)/shard_map/all_gather | solution.py:84
  227.7 2.4 fusion.36
  230.3 1.6 fusion.70
  234.1 2.9 fusion.21
  237.3 1.6 reshape_squeeze.11
  238.9 1.6 reshape_squeeze.10
  240.4 3.3 fusion.5
  243.7 6.5 fusion.12
  250.2 1.7 copy.53
  251.9 1.1 fusion.10
  253.0 79.7 %all-gather.14.cloned.1.call-done = bf16[1,2048,512]{1,2,0:T(8,128)(2,1)} async-done(((bf16[1,128,512]{1,2,0:T(8,128)(2,1)}), bf16[1,2048,512]{1,2,0:T(8,128)(2,1)}) %all-gather.14.cloned.1.call-update) | async-done | bytes 2097168 | tf_op jit(solution)/shard_map/all_gather | solution.py:125
  332.7 4.6 fusion.32
  337.2 99.0 %all-gather.8.cloned.1.call-done = bf16[2048,512]{1,0:T(8,128)(2,1)} async-done(((bf16[128,512]{1,0:T(8,128)(2,1)}), bf16[2048,512]{1,0:T(8,128)(2,1)}) %all-gather.8.cloned.1.call-update) | async-done | bytes 2097168 | tf_op jit(solution)/shard_map/all_gather | solution.py:126
  436.2 3.9 copy.59
  440.1 6.0 fusion.11
  446.1 116.6 %reduce-scatter.2.cloned.1.call-done = f32[16,1024]{1,0:T(8,128)} async-done(((f32[512,1024]{1,0:T(8,128)}), f32[16,1024]{1,0:T(8,128)}) %reduce-scatter.2.cloned.1.call-update) | async-done | bytes 65552 | tf_op jit(solution)/shard_map/reduce_scatter | solution.py:164
  562.8 4.8 fusion.13
  569.1 206.6 %all-reduce.2.cloned.1.call-done = f32[16,1024]{1,0:T(8,128)} async-done(((f32[16,1024]{1,0:T(8,128)}), f32[16,1024]{1,0:T(8,128)}) %all-reduce.2.cloned.1.call-update) | async-done | bytes 65552 | tf_op jit(solution)/shard_map/psum | solution.py:163
  775.7 1.5 copy.74
  (68 shorter events, 7.8 us)
Async XLA Ops:
  7.2 225.2 %copy-start = (bf16[512,1024]{1,0:T(8,128)(2,1)S(1)}, bf16[512,1024]{1,0:T(8,128)(2,1)}, u32[]{:S(2)}) copy-start(bf16[512,1024]{1,0:T(8,128)(2,1)} %param.14) | copy-start | bytes 3145732
  7.2 115.1 %all-gather.12.cloned.1.call-start = ((), (), s32[]{:S(2)}) async-start(), calls=%async_computation.3 | async-start | bytes 2228224 | tf_op jit(solution)/shard_map/all_gather | solution.py:85
  7.9 219.8 %all-gather.10.cloned.1.call-start = ((), (), s32[]{:S(2)}) async-start(), calls=%async_computation.2 | async-start | bytes 2228224 | tf_op jit(solution)/shard_map/all_gather | solution.py:84
  9.7 323.0 %all-gather.14.cloned.1.call-start = ((), (), s32[]{:S(2)}) async-start(), calls=%async_computation.4 | async-start | bytes 2228224 | tf_op jit(solution)/shard_map/all_gather | solution.py:125
  11.4 424.8 %all-gather.8.cloned.1.call-start = ((), (), s32[]{:S(2)}) async-start(), calls=%async_computation.1 | async-start | bytes 2228224 | tf_op jit(solution)/shard_map/all_gather | solution.py:126
  14.1 216.1 %copy-start.13 = (s32[128]{0:T(128)}, s32[128]{0:T(128)S(1)}, u32[]{:S(2)}) copy-start(s32[128]{0:T(128)S(1)} %select_reduce_fusion.1) | copy-start | bytes 1540
  14.1 216.1 %copy-start.14 = (s32[128]{0:T(128)}, s32[128]{0:T(128)S(1)}, u32[]{:S(2)}) copy-start(s32[128]{0:T(128)S(1)} %fusion.61) | copy-start | bytes 1540
  14.2 216.0 %copy-start.15 = (s32[128]{0:T(128)}, s32[128]{0:T(128)S(1)}, u32[]{:S(2)}) copy-start(s32[128]{0:T(128)S(1)} %convert_reduce_fusion.1) | copy-start | bytes 1540
  14.4 215.8 %copy-start.12 = (s32[2048]{0:T(1024)}, s32[2048]{0:T(1024)S(1)}, u32[]{:S(2)}) copy-start(s32[2048]{0:T(1024)S(1)} %convert_reduce_fusion) | copy-start | bytes 24580
  16.0 214.3 %copy-start.16 = (f32[128,2048]{1,0:T(8,128)}, f32[128,2048]{1,0:T(8,128)S(1)}, u32[]{:S(2)}) copy-start(f32[128,2048]{1,0:T(8,128)S(1)} %fusion.2) | copy-start | bytes 3145732
  227.7 2.5 copy-start.5
  230.2 1.9 copy-start.1
  230.2 2.2 copy-start.4
  230.3 2.2 copy-start.6
  232.3 1.8 copy-start.8
  232.4 1.6 copy-start.10
  233.9 328.8 %reduce-scatter.2.cloned.1.call-start = ((), (), s32[]{:S(2)}) async-start(), calls=%async_computation.5 | async-start | bytes 2162688 | tf_op jit(solution)/shard_map/reduce_scatter | solution.py:164
  234.1 9.6 %copy-start.3 = (bf16[1,2048,512]{1,2,0:T(8,128)(2,1)S(1)}, bf16[1,2048,512]{1,2,0:T(8,128)(2,1)}, u32[]{:S(2)}) copy-start(bf16[1,2048,512]{1,2,0:T(8,128)(2,1)} %all-gather.10.cloned.1.call-done) | copy-start | bytes 6291460
  237.0 538.7 %all-reduce.2.cloned.1.call-start = ((), (), s32[]{:S(2)}) async-start(), calls=%async_computation.6 | async-start | bytes 131072 | tf_op jit(solution)/shard_map/psum | solution.py:163
  243.7 8.2 %copy-start.9 = (f32[128]{0:T(128)S(1)}, f32[128]{0:T(128)}, u32[]{:S(2)}) copy-start(f32[128]{0:T(128)} %copy-done.8) | copy-start | bytes 1540
  243.7 8.2 %copy-start.11 = (f32[128]{0:T(128)S(1)}, f32[128]{0:T(128)}, u32[]{:S(2)}) copy-start(f32[128]{0:T(128)} %copy-done.10) | copy-start | bytes 1540
  332.7 107.5 %copy-start.2 = (bf16[1,2048,512]{1,2,0:T(8,128)(2,1)S(1)}, bf16[1,2048,512]{1,2,0:T(8,128)(2,1)}, u32[]{:S(2)}) copy-start(bf16[1,2048,512]{1,2,0:T(8,128)(2,1)} %all-gather.14.cloned.1.call-done) | copy-start | bytes 6291460
  332.7 107.5 %copy-start.7 = (bf16[128,4,128]{2,1,0:T(4,128)(2,1)S(1)}, bf16[128,4,128]{2,1,0:T(4,128)(2,1)}, u32[]{:S(2)}) copy-start(bf16[128,4,128]{2,1,0:T(4,128)(2,1)} %reshape_squeeze.10) | copy-start | bytes 393220
Sparse Core Ops, SparseCore 0:
  11.2 111.0 all-gather.11
  125.9 101.7 all-gather.9
  230.8 101.8 all-gather.13
  336.3 99.8 all-gather.7
  438.8 123.8 reduce-scatter.1
  565.8 209.9 all-reduce.1
where the time goes:
time: 785 us; the launch traced here: 784 us
  waiting for transfers between devices  710 us (90%)
  matrix products  35.2 us (4%)
  local copies, waits for them, and re-layouts  20.6 us (3%)
  between operations  14.4 us (2%)
    psum x1, waiting for transfers between devices, body(): group_sum = lax.psum(weight_part, 'seq')  207 us
    reduce_scatter x1, waiting for transfers between devices, body(): lax.psum_scatter(group_sum, 'dp', scatter_dimension=0, tiled=True)  117 us
    all_gather x1, waiting for transfers between devices, body(): value_part = lax.all_gather(value_rows, 'seq', axis=0, tiled=True)  106 us
    all_gather x1, waiting for transfers between devices, body(): key_part = lax.all_gather(key_rows, 'seq', axis=0, tiled=True)  101 us
    all_gather x1, waiting for transfers between devices, body(): peer_grad = lax.all_gather(d_attended, 'seq', axis=0, tiled=True)  99 us
    all_gather x1, waiting for transfers between devices, body(): peer_query = lax.all_gather(query_rows, 'seq', axis=0, tiled=True)  79.7 us
  transfers between devices with their start and end apart: 6, of which 6 were waited for; matrix products, arithmetic and copies ran while one was open for 7% of the time, Pallas kernels for 0%

commit v1 on v0

v1 whole, which is shorter than its diff:
```python
import functools

import jax
import jax.numpy as jnp
from jax import lax
from jax.experimental import pallas as pl
from jax.experimental.pallas import tpu as pltpu
from jax.sharding import PartitionSpec as P

H = 4
DH = 128
T = 128
F32 = jnp.float32
BF16 = jnp.bfloat16
MESH = pl.DeviceIdType.MESH
EPS = 1e-06
NT = (((1,), (1,)), ((), ()))
TN = (((0,), (0,)), ((), ()))
HALF_SCALE = 0.5 * DH ** (-0.5)


def dot(a, b, dims=(((1,), (0,)), ((), ()))):
    return lax.dot_general(a, b, dims, preferred_element_type=F32)


def kernel(
    q_ref, k_ref, v_ref, g_ref, do_ref, w_ref, len_ref, own_ref, pat_ref,
    lo_ref, dq_ref, dk_ref, dv_ref, gg_ref, wg_ref,
    kv_s, q_s, meta_s, meta_r, kv, rq, kt, wt, sl, low, high, att_t, att_s, ratt,
    dgat, gated, da_s, rda, sib_s, sib_r, dkv_s, rdkv, dq_t, dq_s, rdq,
    do_sib, g_t, g_sib, wx_own, wx_s, wx_r, wl_s, wl_r, ws, ws_r, wa_s, wa,
    kv_send, kv_recv, fwd_send, q_send, q_recv, one_send, one_recv, att_send, att_recv,
    da_send, da_recv, sib_send, sib_recv, dkv_send, dkv_recv, dq_send, dq_recv,
    x_send, x_recv, l_send, l_recv, s_send, s_recv, a_send, a_recv,
):
    dp = lax.axis_index("dp")
    sq = lax.axis_index("seq")
    x = lax.div(dp, 8)
    l = lax.rem(lax.div(dp, 2), 4)
    c = lax.rem(dp, 2)
    y = lax.div(sq, 2)
    z = lax.rem(sq, 2)
    par = lax.rem(y, 2)
    hh = lax.div(y, 2)
    sib = (dp + 1 - 2 * c, sq)
    own_par = par == c

    def partner(k, zz):
        return (dp - c + par, (2 * k + c) * 2 + zz)

    def is_self(k, zz):
        return own_par & (k == hh) & (zz == z)

    def remote(src, dst, send, recv, to):
        return pltpu.make_async_remote_copy(
            src_ref=src, dst_ref=dst, send_sem=send, recv_sem=recv, device_id=to,
            device_id_type=MESH,
        )

    def arrived(dst, sem):
        pltpu.make_async_copy(dst, dst, sem).wait()

    def push(src, dst, send, recv, k, zz):
        me = is_self(k, zz)

        @pl.when(jnp.logical_not(me))
        def _():
            remote(src, dst, send, recv, partner(k, zz)).start()

        @pl.when(me)
        def _():
            pltpu.make_async_copy(src, dst, recv).start()

    def pushed(src, dst, send, recv, k, zz):
        @pl.when(jnp.logical_not(is_self(k, zz)))
        def _():
            remote(src, dst, send, recv, partner(k, zz)).wait_send()

    def x_dev(i):
        return (lax.rem(x + i, 4) * 8 + l * 2 + c, sq)

    def l_dev(i):
        return (x * 8 + lax.rem(l + i, 4) * 2 + c, sq)

    def s_dev(i):
        return (dp, lax.rem(sq + i, 16))

    barrier = pltpu.get_barrier_semaphore()

    def tell(to):
        pl.semaphore_signal(barrier, inc=1, device_id=to, device_id_type=MESH)

    for k in range(4):
        for zz in range(2):
            @pl.when(jnp.logical_not(is_self(k, zz)))
            def _():
                tell(partner(k, zz))
    tell(sib)
    for i in range(1, 4):
        tell(x_dev(i))
        tell(l_dev(i))
    for i in range(1, 16):
        tell(s_dev(i))

    for h in range(H):
        cols = slice(h * DH, (h + 1) * DH)
        kv_s[h, 0] = k_ref[0, :, cols]
        kv_s[h, 1] = v_ref[0, :, cols]
        q_s[h] = q_ref[0, :, cols]
    meta_s[...] = jnp.zeros_like(meta_s)
    meta_s[0:1, 0:4] = len_ref[...].astype(F32)
    meta_s[1:2, 0:16] = own_ref[...].astype(F32)
    meta_s[8:24, 0:16] = pat_ref[0].astype(F32)

    pl.semaphore_wait(barrier, 30 - jnp.where(own_par, 1, 0))

    meta_copy = remote(meta_s, meta_r, one_send.at[0], one_recv.at[0], sib)
    meta_copy.start()

    def place(i):
        step = lax.rem(i, 4)
        turn = jnp.where(step == 2, 3, jnp.where(step == 3, 2, step))
        return lax.rem(hh + turn, 4), jnp.where(i < 4, z, 1 - z)

    for k in range(4):
        push(q_s.at[k], rq.at[hh], q_send.at[k], q_recv.at[hh], k, z)
    for zz in (1 - z, z):
        for k in range(4):
            push(kv_s.at[k], kv.at[sq], kv_send.at[2 * k + zz], kv_recv.at[sq], k, zz)
    do_copy = remote(do_ref.at[0], do_sib, one_send.at[1], one_recv.at[1], sib)
    do_copy.start()

    dgat[...] = dot(do_ref[0], w_ref[...], NT)

    meta_copy.wait()
    meta = jnp.where(own_par, meta_s[...], meta_r[...])
    lane = lax.broadcasted_iota(jnp.int32, (16, 128), 1).astype(F32)
    seat = lax.broadcasted_iota(jnp.int32, (16, 128), 0).astype(F32)
    hot = jnp.where((meta[1:2] == seat) & (lane < 16), 1.0, 0.0)
    tile = jnp.sum(hot * lane, axis=1, keepdims=True)
    col = lax.broadcasted_iota(jnp.int32, (16, 512), 1)
    row = lax.broadcasted_iota(jnp.int32, (16, 512), 0)
    query_hot = jnp.where(row == 4 * lax.div(col, 128) + 2 * c + z, 1.0, 0.0)
    query_tile = jnp.sum(tile * query_hot, axis=0, keepdims=True)
    pos = query_tile * T + lax.rem(col, 128)[0:1].astype(F32)
    lengths = jnp.where((lane[0:8] <= seat[0:8]) & (lane[0:8] < 4), meta[0:1], 0.0)
    ends = jnp.sum(lengths, axis=1, keepdims=True)
    first = jnp.max(jnp.where(ends <= pos, ends, 0.0), axis=0, keepdims=True)
    tile_hot = jnp.where(row.astype(F32) == query_tile, 1.0, 0.0)
    seen = dot(meta[8:24], tile_hot, TN)
    allow = (dot(hot, seen) > 0.5) | (tile == query_tile)
    low[...] = jnp.where(allow, first - tile * T, 1e6)
    high[...] = pos - tile * T

    for k in range(4):
        arrived(rq.at[k], q_recv.at[k])

    att_t[...] = jnp.zeros_like(att_t)

    def attend(s):
        keys = kv[s, 0]
        values_t = kv[s, 1].T
        kt[s] = keys.T
        key_at = lax.broadcasted_iota(jnp.int32, (T, 256), 0).astype(F32)
        for j in range(2):
            cols = slice(j * 256, (j + 1) * 256)
            part = dot(keys, rq[2 * j : 2 * j + 2].reshape(256, DH), NT) * HALF_SCALE
            keep = (key_at >= low[pl.ds(s, 1), cols]) & (key_at <= high[pl.ds(s, 1), cols])
            tan = jnp.tanh(part)
            up = 1.0 + tan
            weights = jnp.where(keep, part * up, 0.0).astype(BF16)
            slope = up * (1.0 + part * (1.0 - tan)) * HALF_SCALE
            wt[s, :, cols] = weights
            sl[s, :, cols] = jnp.where(keep, slope, 0.0)
            att_t[:, cols] += dot(values_t, weights)

    def forward_step(i, _):
        k, zz = place(i)
        mine = (2 * k + c) * 2 + zz
        arrived(kv.at[mine], kv_recv.at[mine])
        remote(kv.at[mine], kv.at[mine], fwd_send.at[i], kv_recv.at[mine], sib).start()
        attend(mine)
        other = (2 * k + 1 - c) * 2 + zz
        arrived(kv.at[other], kv_recv.at[other])
        attend(other)
        return 0

    lax.fori_loop(0, 8, forward_step, 0)

    for k in range(4):
        att_s[k] = att_t[:, k * T : (k + 1) * T].T
        push(att_s.at[k], ratt.at[hh], att_send.at[k], att_recv.at[hh], k, z)

    for h in range(H):
        arrived(ratt.at[h], att_recv.at[h])
    rows = [ratt[h] for h in range(H)]
    mean = sum(jnp.sum(r, axis=1, keepdims=True) for r in rows) * (1.0 / 512)
    rows = [r - mean for r in rows]
    var = sum(jnp.sum(r * r, axis=1, keepdims=True) for r in rows) * (1.0 / 512)
    inv = lax.rsqrt(var + EPS)
    normed = [r * inv for r in rows]
    d_normed = []
    for h in range(H):
        cols = slice(h * DH, (h + 1) * DH)
        gates = g_ref[0, :, cols].astype(F32)
        d_gated = dgat[:, cols]
        gated[:, cols] = (normed[h] * gates).astype(BF16)
        gg_ref[0, :, cols] = (d_gated * normed[h]).astype(BF16)
        d_normed.append(d_gated * gates)
    mean_d = sum(jnp.sum(d, axis=1, keepdims=True) for d in d_normed) * (1.0 / 512)
    mean_dn = sum(
        jnp.sum(d * n, axis=1, keepdims=True) for d, n in zip(d_normed, normed)
    ) * (1.0 / 512)
    for h in range(H):
        da_s[h] = ((d_normed[h] - mean_d - normed[h] * mean_dn) * inv).astype(BF16)
        push(da_s.at[h], rda.at[hh], da_send.at[h], da_recv.at[hh], h, z)

    for h in range(H):
        g_t[4 * h : 4 * h + 4] = gated[:, h * DH : (h + 1) * DH].T.reshape(4, 2, 16, T)
    g_copy = remote(g_t.at[:, 1 - c], g_sib, one_send.at[2], one_recv.at[2], sib)
    g_copy.start()
    lo_ref[0] = dot(gated[...], w_ref[...]).astype(BF16)
    do_copy.wait()
    g_copy.wait()
    mine_t = g_t[:, pl.ds(c, 1)].reshape(256, T)
    theirs_t = g_sib[...].reshape(256, T)
    part = dot(mine_t, do_ref[0]) + dot(theirs_t, do_sib[...])
    wx_own[...] = part.reshape(4, 64, 1024)
    wx_s[...] = part.astype(BF16).reshape(4, 64, 1024)
    for i in range(1, 4):
        there = lax.rem(x + i, 4)
        remote(wx_s.at[there], wx_r.at[i - 1], x_send.at[i - 1], x_recv.at[i - 1], x_dev(i)).start()

    for k in range(4):
        arrived(rda.at[k], da_recv.at[k])
    dq_t[...] = jnp.zeros_like(dq_t)

    def back(s):
        values = kv[s, 1]
        d_keys = jnp.zeros((T, DH), F32)
        d_values = jnp.zeros((T, DH), F32)
        for j in range(2):
            cols = slice(j * 256, (j + 1) * 256)
            grads = rda[2 * j : 2 * j + 2].reshape(256, DH)
            d_scores = (dot(values, grads, NT) * sl[s, :, cols]).astype(BF16)
            d_keys += dot(d_scores, rq[2 * j : 2 * j + 2].reshape(256, DH))
            d_values += dot(wt[s, :, cols], grads)
            dq_t[:, cols] += dot(kt[s], d_scores)
        return d_keys, d_values

    def back_other(i, _):
        k, zz = place(7 - i)
        d_keys, d_values = back((2 * k + 1 - c) * 2 + zz)
        sib_s[i, 0] = d_keys.astype(BF16)
        sib_s[i, 1] = d_values.astype(BF16)
        remote(sib_s.at[i], sib_r.at[i], sib_send.at[i], sib_recv.at[i], sib).start()
        return 0

    def back_mine(i, _):
        k, zz = place(7 - i)
        d_keys, d_values = back((2 * k + c) * 2 + zz)
        arrived(sib_r.at[i], sib_recv.at[i])
        dkv_s[i, 0] = (d_keys + sib_r[i, 0].astype(F32)).astype(BF16)
        dkv_s[i, 1] = (d_values + sib_r[i, 1].astype(F32)).astype(BF16)
        push(dkv_s.at[i], rdkv.at[z, hh], dkv_send.at[i], dkv_recv.at[4 * z + hh], k, zz)
        return 0

    lax.fori_loop(0, 8, back_other, 0)
    lax.fori_loop(0, 8, back_mine, 0)
    for k in range(4):
        dq_s[k] = dq_t[:, k * T : (k + 1) * T].T.astype(BF16)
        push(dq_s.at[k], rdq.at[hh], dq_send.at[k], dq_recv.at[hh], k, z)

    for i in range(3):
        arrived(wx_r.at[i], x_recv.at[i])
    total = wx_own[x]
    for i in range(3):
        total += wx_r[i].astype(F32)
    wl_s[...] = total.reshape(4, 16, 1024)
    for i in range(1, 4):
        there = lax.rem(l + i, 4)
        remote(wl_s.at[there], wl_r.at[i - 1], l_send.at[i - 1], l_recv.at[i - 1], l_dev(i)).start()
    for i in range(3):
        arrived(wl_r.at[i], l_recv.at[i])
    ws[...] = wl_s[l] + wl_r[0] + wl_r[1] + wl_r[2]

    def piece(ref, s):
        down = pl.multiple_of(lax.div(s, 8) * 8, 8)
        across = pl.multiple_of(lax.rem(s, 8) * 128, 128)
        return ref.at[pl.ds(down, 8), pl.ds(across, 128)]

    def spread(i, _):
        there = lax.rem(sq + i, 16)
        remote(piece(ws, there), ws_r.at[i], s_send.at[i], s_recv.at[i], s_dev(i)).start()
        return 0

    lax.fori_loop(1, 16, spread, 0)
    pltpu.make_async_copy(piece(ws, sq), ws_r.at[0], s_recv.at[0]).start()

    def fold(i, acc):
        arrived(ws_r.at[i], s_recv.at[i])
        return acc + ws_r[i]

    wa_s[...] = lax.fori_loop(0, 16, fold, jnp.zeros((8, 128), F32))

    def share(i, _):
        remote(wa_s, piece(wa, sq), a_send.at[i], a_recv.at[sq], s_dev(i)).start()
        return 0

    lax.fori_loop(1, 16, share, 0)
    pltpu.make_async_copy(wa_s, piece(wa, sq), a_recv.at[sq]).start()

    for h in range(H):
        cols = slice(h * DH, (h + 1) * DH)
        arrived(rdq.at[h], dq_recv.at[h])
        dq_ref[0, :, cols] = rdq[h]
    for h in range(H):
        cols = slice(h * DH, (h + 1) * DH)
        arrived(rdkv.at[0, h], dkv_recv.at[h])
        arrived(rdkv.at[1, h], dkv_recv.at[4 + h])
        dk_ref[0, :, cols] = (rdkv[0, h, 0].astype(F32) + rdkv[1, h, 0].astype(F32)).astype(BF16)
        dv_ref[0, :, cols] = (rdkv[0, h, 1].astype(F32) + rdkv[1, h, 1].astype(F32)).astype(BF16)

    def gathered(i, _):
        arrived(piece(wa, i), a_recv.at[i])
        return 0

    lax.fori_loop(0, 16, gathered, 0)
    wg_ref[...] = wa[...]

    for k in range(4):
        pushed(q_s.at[k], rq.at[hh], q_send.at[k], q_recv.at[hh], k, z)
        pushed(att_s.at[k], ratt.at[hh], att_send.at[k], att_recv.at[hh], k, z)
        pushed(da_s.at[k], rda.at[hh], da_send.at[k], da_recv.at[hh], k, z)
        pushed(dq_s.at[k], rdq.at[hh], dq_send.at[k], dq_recv.at[hh], k, z)
        for zz in range(2):
            pushed(kv_s.at[k], kv.at[sq], kv_send.at[2 * k + zz], kv_recv.at[sq], k, zz)

    def left(i, _):
        k, zz = place(i)
        mine = (2 * k + c) * 2 + zz
        remote(kv.at[mine], kv.at[mine], fwd_send.at[i], kv_recv.at[mine], sib).wait_send()
        remote(sib_s.at[i], sib_r.at[i], sib_send.at[i], sib_recv.at[i], sib).wait_send()
        k, zz = place(7 - i)
        pushed(dkv_s.at[i], rdkv.at[z, hh], dkv_send.at[i], dkv_recv.at[4 * z + hh], k, zz)
        return 0

    lax.fori_loop(0, 8, left, 0)
    for i in range(1, 4):
        remote(wx_s.at[i], wx_r.at[i - 1], x_send.at[i - 1], x_recv.at[i - 1], x_dev(i)).wait_send()
        remote(wl_s.at[i], wl_r.at[i - 1], l_send.at[i - 1], l_recv.at[i - 1], l_dev(i)).wait_send()

    def left_seq(i, _):
        remote(wa_s, ws_r.at[i], s_send.at[i], s_recv.at[i], s_dev(i)).wait_send()
        remote(wa_s, ws_r.at[i], a_send.at[i], a_recv.at[i], s_dev(i)).wait_send()
        return 0

    lax.fori_loop(1, 16, left_seq, 0)


def body(queries, keys, values, gates, d_out, w_out, lengths, tile_owner, pattern):
    vmem = pl.BlockSpec(memory_space=pltpu.VMEM)
    rows = jax.ShapeDtypeStruct((1, T, 512), BF16)
    dma = pltpu.SemaphoreType.DMA
    buf = pltpu.VMEM
    scratch = dict(
        kv_s=buf((4, 2, T, DH), BF16), q_s=buf((4, T, DH), BF16),
        meta_s=buf((24, 128), F32), meta_r=buf((24, 128), F32),
        kv=buf((16, 2, T, DH), BF16), rq=buf((4, T, DH), BF16), kt=buf((16, DH, T), BF16),
        wt=buf((16, T, 512), BF16), sl=buf((16, T, 512), F32),
        low=buf((16, 512), F32), high=buf((16, 512), F32),
        att_t=buf((DH, 512), F32), att_s=buf((4, T, DH), F32), ratt=buf((4, T, DH), F32),
        dgat=buf((T, 512), F32), gated=buf((T, 512), BF16),
        da_s=buf((4, T, DH), BF16), rda=buf((4, T, DH), BF16),
        sib_s=buf((8, 2, T, DH), BF16), sib_r=buf((8, 2, T, DH), BF16),
        dkv_s=buf((8, 2, T, DH), BF16), rdkv=buf((2, 4, 2, T, DH), BF16),
        dq_t=buf((DH, 512), F32), dq_s=buf((4, T, DH), BF16), rdq=buf((4, T, DH), BF16),
        do_sib=buf((T, 1024), BF16), g_t=buf((16, 2, 16, T), BF16), g_sib=buf((16, 16, T), BF16),
        wx_own=buf((4, 64, 1024), F32), wx_s=buf((4, 64, 1024), BF16), wx_r=buf((3, 64, 1024), BF16),
        wl_s=buf((4, 16, 1024), F32), wl_r=buf((3, 16, 1024), F32),
        ws=buf((16, 1024), F32), ws_r=buf((16, 8, 128), F32),
        wa_s=buf((8, 128), F32), wa=buf((16, 1024), F32),
        kv_send=dma((8,)), kv_recv=dma((16,)), fwd_send=dma((8,)), q_send=dma((4,)), q_recv=dma((4,)),
        one_send=dma((3,)), one_recv=dma((3,)), att_send=dma((4,)), att_recv=dma((4,)),
        da_send=dma((4,)), da_recv=dma((4,)), sib_send=dma((8,)), sib_recv=dma((8,)),
        dkv_send=dma((8,)), dkv_recv=dma((8,)), dq_send=dma((4,)), dq_recv=dma((4,)),
        x_send=dma((3,)), x_recv=dma((3,)), l_send=dma((3,)), l_recv=dma((3,)),
        s_send=dma((16,)), s_recv=dma((16,)), a_send=dma((16,)), a_recv=dma((16,)),
    )
    return pl.pallas_call(
        kernel,
        out_shape=(
            jax.ShapeDtypeStruct((1, T, 1024), BF16), rows, rows, rows, rows,
            jax.ShapeDtypeStruct((16, 1024), F32),
        ),
        in_specs=[vmem] * 9,
        out_specs=(vmem,) * 6,
        scratch_shapes=list(scratch.values()),
        name="hstu",
        compiler_params=pltpu.CompilerParams(
            collective_id=0, has_side_effects=True, vmem_limit_bytes=48 << 20
        ),
    )(queries, keys, values, gates, d_out, w_out, lengths, tile_owner, pattern)


def solution(mesh):
    rows = P("dp", "seq", None)
    in_specs = (rows, rows, rows, rows, rows, P(), P("dp", None), P("dp", None), P("dp", None, None))
    out_specs = (rows, rows, rows, rows, rows, P("dp", None))
    return jax.shard_map(body, mesh=mesh, in_specs=in_specs, out_specs=out_specs, check_vma=False)
```

time: 785 us -> 111 us (0.14)
  waiting for transfers between devices: 710 us -> 0 us
  Pallas kernels: 0 us -> 98.4 us
  matrix products: 35.2 us -> 0 us
  between operations: 14.4 us -> 0.66 us
  local copies, waits for them, and re-layouts: 20.6 us -> 11.7 us
    all_gather x4 -> x0, waiting for transfers between devices: 386 us -> none  [the longest x1 106 us: body(): value_part = lax.all_gather(value_rows, 'seq', axis=0, tiled=True)]
    psum x1 -> x0, waiting for transfers between devices: 207 us -> none  [body(): group_sum = lax.psum(weight_part, 'seq')]
    reduce_scatter x1 -> x0, waiting for transfers between devices: 117 us -> none  [body(): lax.psum_scatter(group_sum, 'dp', scatter_dimension=0, tiled=True)]
    pallas_call x0 -> x1, Pallas kernels: none -> 98.4 us  [body(): pl.pallas_call(kernel, out_shape=(jax.ShapeDtypeStruct((1, T, 1024), BF16...]
    dot_general x11 -> x0, matrix products: 35.2 us -> none  [the longest x1 6.48 us: body(): jnp.einsum('hqk,khd->qhd', d_scores, key_part_heads, preferred_element_ty...]
  transfers between devices with their start and end apart: 6 -> 0, of which waited for: 6 -> 0; matrix products, arithmetic and copies ran while one was open for 7% -> 0% of each run, Pallas kernels for 0% -> 0%
where the time goes in v1:
time: 111 us
  Pallas kernels  98.4 us (89%)
  local copies, waits for them, and re-layouts  11.7 us (11%)
    pallas_call x1, Pallas kernels, body(): pl.pallas_call(kernel, out_shape=(jax.ShapeDtypeStruct((1, T, 1024), BF16...  98.4 us
    unnamed x24, local copies, waits for them, and re-layouts  11.7 us

profile of v1, /device:TPU:6, one launch (start us, length us, event | category | flops | bytes accessed | tf_op | source)
XLA Modules:
  0.0 110.8 jit_solution(10631324049172711211)
XLA Ops:
  0.6 0.0 copy-start
  0.6 1.2 %copy-done = bf16[512,1024]{1,0:T(8,128)(2,1)S(1)} copy-done((bf16[512,1024]{1,0:T(8,128)(2,1)S(1)}, bf16[512,1024]{1,0:T(8,128)(2,1)}, u32[]{:S(2)}) %copy-start) | copy-done | bytes 1048600
  1.9 0.0 copy-start.1
  1.9 0.9 copy-done.1
  2.8 0.0 copy-start.2
  2.8 0.9 copy-done.2
  3.7 0.0 copy-start.3
  3.7 0.9 copy-done.3
  4.6 0.0 copy-start.4
  4.6 0.9 copy-done.4
  5.5 0.0 copy-start.5
  5.5 0.9 copy-done.5
  6.4 0.0 copy-start.6
  6.4 0.7 copy-done.6
  7.1 0.0 copy-start.7
  7.1 0.7 copy-done.7
  7.8 0.7 copy-done.8
  8.4 98.4 %hstu.1 = (bf16[1,128,1024]{2,1,0:T(8,128)(2,1)S(1)}, bf16[1,128,512]{2,1,0:T(8,128)(2,1)S(1)}, bf16[1,128,512]{2,1,0:T(8,128)(2,1)S(1)}, bf16[1,128,512]{2,1,0:...) custom-call(bf16[1,128,512]{2,1,0:T(8,128)(2,1)S(1)} %copy-done.2, ...), custom_call_target="tpu_custom_call" | custom-call | tf_op jit(solution)/shard_map/hstu/pallas_call | solution.py:390
  106.8 0.7 copy.21
  107.5 0.7 copy.22
  108.2 0.7 copy.23
  108.8 0.7 copy.24
  109.5 0.7 copy.25
  110.1 0.6 copy.26
  (1 shorter events, 0.0 us)
Async XLA Ops:
  0.6 1.2 %copy-start = (bf16[512,1024]{1,0:T(8,128)(2,1)S(1)}, bf16[512,1024]{1,0:T(8,128)(2,1)}, u32[]{:S(2)}) copy-start(bf16[512,1024]{1,0:T(8,128)(2,1)} %w_ref.1) | copy-start | bytes 3145732
  1.9 0.9 copy-start.1
  2.8 0.9 copy-start.2
  3.7 0.9 copy-start.3
  4.6 0.9 copy-start.4
  5.5 0.9 copy-start.5
  6.4 0.7 copy-start.6
  7.1 0.7 copy-start.7
  7.8 0.7 copy-start.8

commit v2 on v1

v2 whole, which is shorter than its diff:
```python
import jax
import jax.numpy as jnp
from jax import lax
from jax.experimental import pallas as pl
from jax.experimental.pallas import tpu as pltpu
from jax.sharding import PartitionSpec as P

H = 4
DH = 128
T = 128
F32 = jnp.float32
BF16 = jnp.bfloat16
MESH = pl.DeviceIdType.MESH
EPS = 1e-06
NT = (((1,), (1,)), ((), ()))
TN = (((0,), (0,)), ((), ()))
VMEM = 60 << 20
HALF_SCALE = 0.5 * DH ** (-0.5)


def dot(a, b, dims=(((1,), (0,)), ((), ()))):
    return lax.dot_general(a, b, dims, preferred_element_type=F32)


def kernel(
    q_ref, k_ref, v_ref, g_ref, do_ref, w_ref, len_ref, own_ref, pat_ref,
    lo_out, dq_out, dk_out, dv_out, gg_out, wg_out,
    lo_v, dq_v, dk_v, dv_v, gg_v, kv_s, q_s, g_v, w_v, len_v, own_v, pat_v,
    meta_s, meta_r, kv, rq, kt, wt, sl, low, high, att_t, att_s, ratt,
    dgat, gate_t, gated_t, gg_t, da_s, rda, dkv_f, sib_s, sib_r, dkv_s, rdkv, dq_t, dq_s, rdq,
    dox, g_t, gx, wl_f, wl_s, wl_r, ws, ws_r, wa_s, wa,
    in_sem, out_sem, kv_send, kv_recv, fwd_send, q_send, q_recv, meta_sem, att_send, att_recv,
    da_send, da_recv, sib_send, sib_recv, dkv_send, dkv_recv, dq_send, dq_recv,
    do_send, do_recv, g_send, g_recv, l_send, l_recv, s_send, s_recv, a_send, a_recv,
):
    dp = lax.axis_index("dp")
    sq = lax.axis_index("seq")
    x = lax.div(dp, 8)
    l = lax.rem(lax.div(dp, 2), 4)
    c = lax.rem(dp, 2)
    y = lax.div(sq, 2)
    z = lax.rem(sq, 2)
    par = lax.rem(y, 2)
    hh = lax.div(y, 2)
    xc = x * 2 + c
    sib = (dp + 1 - 2 * c, sq)
    own_par = par == c
    own_rows = pl.ds(pl.multiple_of(c * T, T), T)
    sib_rows = pl.ds(pl.multiple_of((1 - c) * T, T), T)
    my_rows = pl.ds(pl.multiple_of(par * T, T), T)

    def partner(k, far):
        return (dp - c + par, (2 * k + c) * 2 + jnp.where(far, 1 - z, z))

    def is_self(k, far):
        return own_par & (k == hh) & jnp.logical_not(far)

    def remote(src, dst, send, recv, to):
        return pltpu.make_async_remote_copy(
            src_ref=src, dst_ref=dst, send_sem=send, recv_sem=recv, device_id=to,
            device_id_type=MESH,
        )

    def arrived(dst, sem):
        pltpu.make_async_copy(dst, dst, sem).wait()

    def push(src, dst, send, recv, k, far=False):
        if far is True:
            remote(src, dst, send, recv, partner(k, far)).start()
            return
        me = is_self(k, far)

        @pl.when(jnp.logical_not(me))
        def _():
            remote(src, dst, send, recv, partner(k, far)).start()

        @pl.when(me)
        def _():
            pltpu.make_async_copy(src, dst, recv).start()

    def pushed(src, dst, send, recv, k, far=False):
        @pl.when(jnp.logical_not(is_self(k, far)))
        def _():
            remote(src, dst, send, recv, partner(k, far)).wait_send()

    def x_dev(i, cc):
        return (lax.rem(x + i, 4) * 8 + l * 2 + cc, sq)

    def l_dev(i):
        return (x * 8 + lax.rem(l + i, 4) * 2 + c, sq)

    def s_dev(i):
        return (dp, lax.rem(sq + i, 16))

    loads = []

    def load(src, dst):
        copy = pltpu.make_async_copy(src, dst, in_sem.at[len(loads)])
        copy.start()
        loads.append(copy)

    load(len_ref, len_v)
    load(own_ref, own_v)
    load(pat_ref, pat_v)
    for h in range(H):
        cols = pl.ds(h * DH, DH)
        load(q_ref.at[0, :, cols], q_s.at[h])
        load(k_ref.at[0, :, cols], kv_s.at[h, 0])
        load(v_ref.at[0, :, cols], kv_s.at[h, 1])
    load(do_ref.at[0], dox.at[xc])
    load(w_ref, w_v)
    load(g_ref.at[0], g_v)

    barrier = pltpu.get_barrier_semaphore()

    def tell(to):
        pl.semaphore_signal(barrier, inc=1, device_id=to, device_id_type=MESH)

    for k in range(4):
        tell(partner(k, True))
        @pl.when(jnp.logical_not(is_self(k, False)))
        def _():
            tell(partner(k, False))
    tell(sib)
    for i in range(1, 4):
        tell(x_dev(i, c))
        tell(x_dev(i, 1 - c))
        tell(l_dev(i))
    for i in range(1, 16):
        tell(s_dev(i))

    for copy in loads[:3]:
        copy.wait()
    meta_s[...] = jnp.zeros_like(meta_s)
    meta_s[0:1, 0:4] = len_v[...].astype(F32)
    meta_s[1:2, 0:16] = own_v[...].astype(F32)
    meta_s[8:24, 0:16] = pat_v[0].astype(F32)
    for copy in loads[3:15]:
        copy.wait()

    pl.semaphore_wait(barrier, 33 - jnp.where(own_par, 1, 0))

    meta_copy = remote(meta_s, meta_r, meta_sem.at[0], meta_sem.at[1], sib)
    meta_copy.start()
    for k in range(4):
        push(q_s.at[k], rq.at[hh], q_send.at[k], q_recv.at[hh], k)
    for k in range(4):
        push(kv_s.at[k], kv.at[4 + hh, :, my_rows], kv_send.at[4 + k], kv_recv.at[8 + y], k, True)
        push(kv_s.at[k], kv.at[hh, :, my_rows], kv_send.at[k], kv_recv.at[y], k)
    for copy in loads[15:]:
        copy.wait()
    remote(dox.at[xc], dox.at[xc], do_send.at[0], do_recv.at[xc], sib).start()
    for i in range(1, 4):
        remote(dox.at[xc], dox.at[xc], do_send.at[i], do_recv.at[xc], x_dev(i, c)).start()

    def place(i):
        step = lax.rem(i, 4)
        turn = jnp.where(step == 2, 3, jnp.where(step == 3, 2, step))
        return lax.rem(hh + turn, 4), lax.div(i, 4)

    dgat[...] = dot(w_v[...], dox[xc], NT)
    for h in range(H):
        gate_t[h * DH : (h + 1) * DH] = g_v[:, h * DH : (h + 1) * DH].T

    meta_copy.wait()
    meta = jnp.where(own_par, meta_s[...], meta_r[...])
    lane = lax.broadcasted_iota(jnp.int32, (16, 128), 1).astype(F32)
    slot = lax.broadcasted_iota(jnp.int32, (16, 128), 0)
    seat = (2 * lax.rem(slot, 8) + jnp.where(slot < 8, z, 1 - z)).astype(F32)
    hot = jnp.where((meta[1:2] == seat) & (lane < 16), 1.0, 0.0)
    tile = jnp.sum(hot * lane, axis=1, keepdims=True)
    col = lax.broadcasted_iota(jnp.int32, (16, 512), 1)
    row = lax.broadcasted_iota(jnp.int32, (16, 512), 0)
    query_hot = jnp.where(row == 2 * lax.div(col, 128) + c, 1.0, 0.0)
    query_tile = jnp.sum(tile * query_hot, axis=0, keepdims=True)
    pos = query_tile * T + lax.rem(col, 128)[0:1].astype(F32)
    upto = slot[0:8].astype(F32)
    lengths = jnp.where((lane[0:8] <= upto) & (lane[0:8] < 4), meta[0:1], 0.0)
    ends = jnp.sum(lengths, axis=1, keepdims=True)
    first = jnp.max(jnp.where(ends <= pos, ends, 0.0), axis=0, keepdims=True)
    tile_hot = jnp.where(row.astype(F32) == query_tile, 1.0, 0.0)
    seen = dot(meta[8:24], tile_hot, TN)
    allow = (dot(hot, seen) > 0.5) | (tile == query_tile)
    low[...] = jnp.where(allow, first - tile * T, 1e6)
    high[...] = pos - tile * T

    for k in range(4):
        arrived(rq.at[k], q_recv.at[k])

    att_t[...] = jnp.zeros_like(att_t)

    def hand_on(i):
        k, far = place(i)
        here = kv.at[4 * far + k, :, own_rows]
        u = 8 * far + 2 * k + c
        arrived(here, kv_recv.at[u])
        remote(here, here, fwd_send.at[i], kv_recv.at[u], sib).start()

    def attend(i):
        k, far = place(i)
        p = 4 * far + k
        u = 8 * far + 2 * k
        arrived(kv.at[p, :, sib_rows], kv_recv.at[u + 1 - c])
        keys = kv[p, 0]
        values_t = kv[p, 1].T
        kt[p] = keys.T
        key_at = lax.broadcasted_iota(jnp.int32, (T, 256), 0).astype(F32)
        for j in range(2):
            cols = slice(j * 256, (j + 1) * 256)
            part = dot(keys, rq[2 * j : 2 * j + 2].reshape(256, DH), NT) * HALF_SCALE
            tan = jnp.tanh(part)
            up = 1.0 + tan
            weights = part * up
            slope = up * (HALF_SCALE + (part * HALF_SCALE) * (1.0 - tan))
            for m in range(2):
                half = slice(m * T, (m + 1) * T)
                keep = (key_at >= low[pl.ds(u + m, 1), cols]) & (key_at <= high[pl.ds(u + m, 1), cols])
                wt[p, half, cols] = jnp.where(keep, weights[half], 0.0).astype(BF16)
                sl[p, half, cols] = jnp.where(keep, slope[half], 0.0)
            att_t[:, cols] += dot(values_t, wt[p, :, cols])

    hand_on(0)

    def forward_step(i, _):
        hand_on(i)
        attend(i - 1)
        return 0

    lax.fori_loop(1, 8, forward_step, 0)
    attend(7)

    for k in range(4):
        block = att_t[:, k * T : (k + 1) * T]
        mean = jnp.sum(block, axis=0, keepdims=True) * (1.0 / DH)
        att_s[k, 0:T] = (block - mean).astype(BF16)
        high_part = mean.astype(BF16)
        rest = mean - high_part.astype(F32)
        mid_part = rest.astype(BF16)
        low_part = (rest - mid_part.astype(F32)).astype(BF16)
        r16 = lax.broadcasted_iota(jnp.int32, (16, T), 0)
        att_s[k, T : T + 16] = jnp.where(
            r16 == 0, high_part.astype(F32),
            jnp.where(r16 == 1, mid_part.astype(F32), jnp.where(r16 == 2, low_part.astype(F32), 0.0)),
        ).astype(BF16)
        push(att_s.at[k], ratt.at[hh], att_send.at[k], att_recv.at[hh], k)

    for i in range(1, 4):
        there = 2 * lax.rem(x + i, 4) + c
        arrived(dox.at[there], do_recv.at[there])
        remote(dox.at[there], dox.at[there], do_send.at[3 + i], do_recv.at[there], sib).start()

    for h in range(H):
        arrived(ratt.at[h], att_recv.at[h])
    rows = []
    for h in range(H):
        tail = jnp.sum(ratt[h, T : T + 16].astype(F32), axis=0, keepdims=True)
        rows.append(ratt[h, 0:T].astype(F32) + tail)
    mean = sum(jnp.sum(r, axis=0, keepdims=True) for r in rows) * (1.0 / 512)
    rows = [r - mean for r in rows]
    var = sum(jnp.sum(r * r, axis=0, keepdims=True) for r in rows) * (1.0 / 512)
    inv = lax.rsqrt(var + EPS)
    normed = [r * inv for r in rows]
    d_normed = []
    for h in range(H):
        feats = slice(h * DH, (h + 1) * DH)
        gates = gate_t[feats].astype(F32)
        d_gated = dgat[feats]
        gated_t[feats] = (normed[h] * gates).astype(BF16)
        gg_t[feats] = (d_gated * normed[h]).astype(BF16)
        d_normed.append(d_gated * gates)
    mean_d = sum(jnp.sum(d, axis=0, keepdims=True) for d in d_normed) * (1.0 / 512)
    mean_dn = sum(
        jnp.sum(d * n, axis=0, keepdims=True) for d, n in zip(d_normed, normed)
    ) * (1.0 / 512)
    for h in range(H):
        da_s[h] = ((d_normed[h] - mean_d - normed[h] * mean_dn) * inv).astype(BF16)
        push(da_s.at[h], rda.at[hh], da_send.at[h], da_recv.at[hh], h)

    for h in range(H):
        blocks = gated_t[h * DH : (h + 1) * DH].reshape(4, 2, 16, T)
        for cc in range(2):
            g_t[h, cc] = blocks[:, cc]
    g_to = [(x_dev(i, (c + cc) % 2 if cc == 0 else 1 - c), i, cc) for i in range(4) for cc in range(2)][1:]
    for n, (to, i, cc) in enumerate(g_to):
        core = c if cc == 0 else 1 - c
        remote(g_t.at[lax.rem(x + i, 4), core], gx.at[xc], g_send.at[n], g_recv.at[xc], to).start()
    gx[xc] = g_t[x, c]
    lo_v[...] = dot(gated_t[...], w_v[...], TN).astype(BF16)
    for h in range(H):
        feats = slice(h * DH, (h + 1) * DH)
        gg_v[:, feats] = gg_t[feats].T
    outs = [
        pltpu.make_async_copy(src, dst, out_sem.at[i])
        for i, (src, dst) in enumerate((
            (lo_v, lo_out.at[0]), (gg_v, gg_out.at[0]), (dq_v, dq_out.at[0]),
            (dk_v, dk_out.at[0]), (dv_v, dv_out.at[0]), (wa, wg_out),
        ))
    ]
    outs[0].start()
    outs[1].start()
    for i in range(4):
        theirs = 2 * lax.rem(x + i, 4) + 1 - c
        arrived(dox.at[theirs], do_recv.at[theirs])
        arrived(gx.at[theirs], g_recv.at[theirs])
        if i:
            arrived(gx.at[theirs + 2 * c - 1], g_recv.at[theirs + 2 * c - 1])
    for n in range(2):
        cols = slice(n * 512, (n + 1) * 512)
        part = dot(gx[0].reshape(64, T), dox[0, :, cols])
        for i in range(1, 8):
            part += dot(gx[i].reshape(64, T), dox[i, :, cols])
        wl_f[:, :, cols] = part.reshape(4, 16, 512)
        wl_s[:, :, cols] = part.astype(BF16).reshape(4, 16, 512)
    for i in range(1, 4):
        there = lax.rem(l + i, 4)
        remote(wl_s.at[there], wl_r.at[i - 1], l_send.at[i - 1], l_recv.at[i - 1], l_dev(i)).start()

    def piece(ref, s):
        down = pl.multiple_of(lax.div(s, 8) * 8, 8)
        across = pl.multiple_of(lax.rem(s, 8) * 128, 128)
        return ref.at[pl.ds(down, 8), pl.ds(across, 128)]

    def spread(i, _):
        there = lax.rem(sq + i, 16)
        remote(piece(ws, there), ws_r.at[i], s_send.at[i], s_recv.at[i], s_dev(i)).start()
        return 0

    for k in range(4):
        arrived(rda.at[k], da_recv.at[k])

    total = wl_f[l]
    for i in range(3):
        arrived(wl_r.at[i], l_recv.at[i])
        total += wl_r[i].astype(F32)
    ws[...] = total
    lax.fori_loop(1, 16, spread, 0)
    pltpu.make_async_copy(piece(ws, sq), ws_r.at[0], s_recv.at[0]).start()

    dq_t[...] = jnp.zeros_like(dq_t)

    def back(i):
        k, far = place(7 - i)
        p = 4 * far + k
        values = kv[p, 1]
        d_keys = jnp.zeros((2 * T, DH), F32)
        d_values = jnp.zeros((2 * T, DH), F32)
        for j in range(2):
            cols = slice(j * 256, (j + 1) * 256)
            grads_t = jnp.concatenate([rda[2 * j], rda[2 * j + 1]], axis=1)
            d_scores = (dot(values, grads_t) * sl[p, :, cols]).astype(BF16)
            d_keys += dot(d_scores, rq[2 * j : 2 * j + 2].reshape(256, DH))
            d_values += dot(wt[p, :, cols], grads_t, NT)
            dq_t[:, cols] += dot(kt[p], d_scores)
        dkv_f[i, 0] = d_keys
        dkv_f[i, 1] = d_values
        sib_s[i, 0] = dkv_f[i, 0, sib_rows].astype(BF16)
        sib_s[i, 1] = dkv_f[i, 1, sib_rows].astype(BF16)
        remote(sib_s.at[i], sib_r.at[i], sib_send.at[i], sib_recv.at[i], sib).start()

    def give(i):
        k, far = place(7 - i)
        arrived(sib_r.at[i], sib_recv.at[i])
        dkv_s[i, 0] = (dkv_f[i, 0, own_rows] + sib_r[i, 0].astype(F32)).astype(BF16)
        dkv_s[i, 1] = (dkv_f[i, 1, own_rows] + sib_r[i, 1].astype(F32)).astype(BF16)
        push(
            dkv_s.at[i], rdkv.at[far, hh], dkv_send.at[i], dkv_recv.at[4 * far + hh], k, far == 1
        )

    back(0)

    def back_step(i, _):
        back(i)
        give(i - 1)
        return 0

    lax.fori_loop(1, 8, back_step, 0)
    for k in range(4):
        dq_s[k] = dq_t[:, k * T : (k + 1) * T].T.astype(BF16)
        push(dq_s.at[k], rdq.at[hh], dq_send.at[k], dq_recv.at[hh], k)
    give(7)

    def fold(i, acc):
        arrived(ws_r.at[i], s_recv.at[i])
        return acc + ws_r[i]

    wa_s[...] = lax.fori_loop(0, 16, fold, jnp.zeros((8, 128), F32))

    def share(i, _):
        remote(wa_s, piece(wa, sq), a_send.at[i], a_recv.at[sq], s_dev(i)).start()
        return 0

    lax.fori_loop(1, 16, share, 0)
    pltpu.make_async_copy(wa_s, piece(wa, sq), a_recv.at[sq]).start()

    for h in range(H):
        cols = slice(h * DH, (h + 1) * DH)
        arrived(rdq.at[h], dq_recv.at[h])
        dq_v[:, cols] = rdq[h]
    outs[2].start()
    for h in range(H):
        cols = slice(h * DH, (h + 1) * DH)
        arrived(rdkv.at[0, h], dkv_recv.at[h])
        arrived(rdkv.at[1, h], dkv_recv.at[4 + h])
        dk_v[:, cols] = (rdkv[0, h, 0].astype(F32) + rdkv[1, h, 0].astype(F32)).astype(BF16)
        dv_v[:, cols] = (rdkv[0, h, 1].astype(F32) + rdkv[1, h, 1].astype(F32)).astype(BF16)

    outs[3].start()
    outs[4].start()

    def gathered(i, _):
        arrived(piece(wa, i), a_recv.at[i])
        return 0

    lax.fori_loop(0, 16, gathered, 0)
    outs[5].start()

    for k in range(4):
        pushed(q_s.at[k], rq.at[hh], q_send.at[k], q_recv.at[hh], k)
        pushed(att_s.at[k], ratt.at[hh], att_send.at[k], att_recv.at[hh], k)
        pushed(da_s.at[k], rda.at[hh], da_send.at[k], da_recv.at[hh], k)
        pushed(dq_s.at[k], rdq.at[hh], dq_send.at[k], dq_recv.at[hh], k)
        pushed(kv_s.at[k], kv.at[hh, :, my_rows], kv_send.at[k], kv_recv.at[y], k)
        remote(kv_s.at[k], kv.at[hh, :, my_rows], kv_send.at[4 + k], kv_recv.at[y], sib).wait_send()

    def left(i, _):
        here = kv.at[0, :, own_rows]
        remote(here, here, fwd_send.at[i], kv_recv.at[0], sib).wait_send()
        remote(sib_s.at[i], sib_r.at[i], sib_send.at[i], sib_recv.at[i], sib).wait_send()
        k, far = place(7 - i)
        pushed(dkv_s.at[i], rdkv.at[0, hh], dkv_send.at[i], dkv_recv.at[hh], k, far == 1)
        return 0

    lax.fori_loop(0, 8, left, 0)
    for i in range(7):
        remote(dox.at[0], dox.at[0], do_send.at[i], do_recv.at[0], sib).wait_send()
        remote(gx.at[0], gx.at[0], g_send.at[i], g_recv.at[0], sib).wait_send()
    for i in range(3):
        remote(wl_s.at[0], wl_r.at[i], l_send.at[i], l_recv.at[i], sib).wait_send()

    def left_seq(i, _):
        remote(wa_s, ws_r.at[i], s_send.at[i], s_recv.at[i], sib).wait_send()
        remote(wa_s, ws_r.at[i], a_send.at[i], a_recv.at[i], sib).wait_send()
        return 0

    lax.fori_loop(1, 16, left_seq, 0)
    for copy in outs:
        copy.wait()


def store(*refs):
    sem = refs[-1]
    copies = [pltpu.make_async_copy(refs[i], refs[6 + i], sem.at[i]) for i in range(6)]
    for copy in copies:
        copy.start()
    for copy in copies:
        copy.wait()


def body(queries, keys, values, gates, d_out, w_out, lengths, tile_owner, pattern):
    hbm = pl.BlockSpec(memory_space=pl.ANY)
    rows = jax.ShapeDtypeStruct((1, T, 512), BF16)
    outs = (
        jax.ShapeDtypeStruct((1, T, 1024), BF16), rows, rows, rows, rows,
        jax.ShapeDtypeStruct((16, 1024), F32),
    )
    dma = pltpu.SemaphoreType.DMA
    buf = pltpu.VMEM
    scratch = dict(
        lo_v=buf((T, 1024), BF16), dq_v=buf((T, 512), BF16), dk_v=buf((T, 512), BF16),
        dv_v=buf((T, 512), BF16), gg_v=buf((T, 512), BF16),
        kv_s=buf((4, 2, T, DH), BF16), q_s=buf((4, T, DH), BF16), g_v=buf((T, 512), BF16),
        w_v=buf((512, 1024), BF16), len_v=buf((1, 4), jnp.int32), own_v=buf((1, 16), jnp.int32),
        pat_v=buf((1, 16, 16), jnp.int32),
        meta_s=buf((24, 128), F32), meta_r=buf((24, 128), F32),
        kv=buf((8, 2, 2 * T, DH), BF16), rq=buf((4, T, DH), BF16), kt=buf((8, DH, 2 * T), BF16),
        wt=buf((8, 2 * T, 512), BF16), sl=buf((8, 2 * T, 512), F32),
        low=buf((16, 512), F32), high=buf((16, 512), F32),
        att_t=buf((DH, 512), F32), att_s=buf((4, T + 16, DH), BF16), ratt=buf((4, T + 16, DH), BF16),
        dgat=buf((512, T), F32), gate_t=buf((512, T), BF16), gated_t=buf((512, T), BF16),
        gg_t=buf((512, T), BF16),
        da_s=buf((4, T, DH), BF16), rda=buf((4, T, DH), BF16), dkv_f=buf((8, 2, 2 * T, DH), F32),
        sib_s=buf((8, 2, T, DH), BF16), sib_r=buf((8, 2, T, DH), BF16),
        dkv_s=buf((8, 2, T, DH), BF16), rdkv=buf((2, 4, 2, T, DH), BF16),
        dq_t=buf((DH, 512), F32), dq_s=buf((4, T, DH), BF16), rdq=buf((4, T, DH), BF16),
        dox=buf((8, T, 1024), BF16), g_t=buf((4, 2, 4, 16, T), BF16), gx=buf((8, 4, 16, T), BF16),
        wl_f=buf((4, 16, 1024), F32), wl_s=buf((4, 16, 1024), BF16), wl_r=buf((3, 16, 1024), BF16),
        ws=buf((16, 1024), F32), ws_r=buf((16, 8, 128), F32),
        wa_s=buf((8, 128), F32), wa=buf((16, 1024), F32),
        in_sem=dma((18,)), out_sem=dma((6,)), kv_send=dma((8,)), kv_recv=dma((16,)), fwd_send=dma((8,)),
        q_send=dma((4,)), q_recv=dma((4,)), meta_sem=dma((2,)), att_send=dma((4,)), att_recv=dma((4,)),
        da_send=dma((4,)), da_recv=dma((4,)), sib_send=dma((8,)), sib_recv=dma((8,)),
        dkv_send=dma((8,)), dkv_recv=dma((8,)), dq_send=dma((4,)), dq_recv=dma((4,)),
        do_send=dma((7,)), do_recv=dma((8,)), g_send=dma((7,)), g_recv=dma((8,)),
        l_send=dma((3,)), l_recv=dma((3,)),
        s_send=dma((16,)), s_recv=dma((16,)), a_send=dma((16,)), a_recv=dma((16,)),
    )
    results = pl.pallas_call(
        kernel,
        out_shape=outs,
        in_specs=[hbm] * 9,
        out_specs=(hbm,) * 6,
        scratch_shapes=list(scratch.values()),
        name="hstu",
        compiler_params=pltpu.CompilerParams(
            collective_id=0, has_side_effects=True, vmem_limit_bytes=VMEM
        ),
    )(queries, keys, values, gates, d_out, w_out, lengths, tile_owner, pattern)
    return pl.pallas_call(
        store,
        out_shape=outs,
        in_specs=[hbm] * 6,
        out_specs=(hbm,) * 6,
        scratch_shapes=[dma((6,))],
        name="store",
        compiler_params=pltpu.CompilerParams(vmem_limit_bytes=VMEM),
    )(*results)


def solution(mesh):
    rows = P("dp", "seq", None)
    in_specs = (rows, rows, rows, rows, rows, P(), P("dp", None), P("dp", None), P("dp", None, None))
    out_specs = (rows, rows, rows, rows, rows, P("dp", None))
    return jax.shard_map(body, mesh=mesh, in_specs=in_specs, out_specs=out_specs, check_vma=False)
```

time: 111 us -> 108 us (0.973)
  the two profiles are of different devices: /device:TPU:6 before, /device:TPU:113 now
where the time goes in v2:
time: 108 us
  Pallas kernels  108 us (100%)
    pallas_call x1, Pallas kernels, body(): pl.pallas_call(kernel, out_shape=outs, in_specs=[hbm] * 9, out_specs=(hbm...  80.7 us
    pallas_call x1, Pallas kernels, body(): pl.pallas_call(store, out_shape=outs, in_specs=[hbm] * 6, out_specs=(hbm,...  27 us

profile of v2, /device:TPU:113, one launch (start us, length us, event | category | flops | bytes accessed | tf_op | source)
XLA Modules:
  0.0 108.3 jit_solution(6444606623625888479)
XLA Ops:
  0.6 80.7 %hstu.1 = (bf16[1,128,1024]{2,1,0:T(8,128)(2,1)}, bf16[1,128,512]{2,1,0:T(8,128)(2,1)}, bf16[1,128,512]{2,1,0:T(8,128)(2,1)}, bf16[1,128,512]{2,1,0:T(8,128)(2,1...) custom-call(bf16[1,128,512]{2,1,0:T(8,128)(2,1)} %q_ref.1, bf16[1,128,512]{2,1,0:T(8,128)(2,1)} %k_ref.1, ...), custom_call_target="tpu_custom_call" | custom-call | tf_op jit(solution)/shard_map/hstu/pallas_call | solution.py:497
  81.3 27.0 %store.1 = (bf16[1,128,1024]{2,1,0:T(8,128)(2,1)}, bf16[1,128,512]{2,1,0:T(8,128)(2,1)}, bf16[1,128,512]{2,1,0:T(8,128)(2,1)}, bf16[1,128,512]{2,1,0:T(8,128)(2,...) custom-call(bf16[1,128,1024]{2,1,0:T(8,128)(2,1)} %get-tuple-element.12.refs_0_, ...), custom_call_target="tpu_custom_call" | custom-call | tf_op jit(solution)/shard_map/store/pallas_call | solution.py:508

commit v3 on v2

--- a/solution.py
+++ b/solution.py
@@ -209,14 +209,12 @@
             cols = slice(j * 256, (j + 1) * 256)
             part = dot(keys, rq[2 * j : 2 * j + 2].reshape(256, DH), NT) * HALF_SCALE
             tan = jnp.tanh(part)
-            up = 1.0 + tan
-            weights = part * up
-            slope = up * (HALF_SCALE + (part * HALF_SCALE) * (1.0 - tan))
+            weights = part + part * tan
+            sl[p, :, cols] = part
             for m in range(2):
                 half = slice(m * T, (m + 1) * T)
                 keep = (key_at >= low[pl.ds(u + m, 1), cols]) & (key_at <= high[pl.ds(u + m, 1), cols])
                 wt[p, half, cols] = jnp.where(keep, weights[half], 0.0).astype(BF16)
-                sl[p, half, cols] = jnp.where(keep, slope[half], 0.0)
             att_t[:, cols] += dot(values_t, wt[p, :, cols])
 
     hand_on(0)
@@ -248,6 +246,22 @@
         there = 2 * lax.rem(x + i, 4) + c
         arrived(dox.at[there], do_recv.at[there])
         remote(dox.at[there], dox.at[there], do_send.at[3 + i], do_recv.at[there], sib).start()
+
+    def slopes(p, _):
+        u = 8 * lax.div(p, 4) + 2 * lax.rem(p, 4)
+        key_at = lax.broadcasted_iota(jnp.int32, (T, 256), 0).astype(F32)
+        for j in range(2):
+            cols = slice(j * 256, (j + 1) * 256)
+            for m in range(2):
+                half = slice(m * T, (m + 1) * T)
+                part = sl[p, half, cols]
+                tan = jnp.tanh(part)
+                slope = (1.0 + tan) * (HALF_SCALE + (part * HALF_SCALE) * (1.0 - tan))
+                keep = (key_at >= low[pl.ds(u + m, 1), cols]) & (key_at <= high[pl.ds(u + m, 1), cols])
+                sl[p, half, cols] = jnp.where(keep, slope, 0.0)
+        return 0
+
+    lax.fori_loop(0, 8, slopes, 0)
 
     for h in range(H):
         arrived(ratt.at[h], att_recv.at[h])
@@ -328,14 +342,6 @@
     for k in range(4):
         arrived(rda.at[k], da_recv.at[k])
 
-    total = wl_f[l]
-    for i in range(3):
-        arrived(wl_r.at[i], l_recv.at[i])
-        total += wl_r[i].astype(F32)
-    ws[...] = total
-    lax.fori_loop(1, 16, spread, 0)
-    pltpu.make_async_copy(piece(ws, sq), ws_r.at[0], s_recv.at[0]).start()
-
     dq_t[...] = jnp.zeros_like(dq_t)
 
     def back(i):
@@ -379,6 +385,14 @@
         push(dq_s.at[k], rdq.at[hh], dq_send.at[k], dq_recv.at[hh], k)
     give(7)
 
+    total = wl_f[l]
+    for i in range(3):
+        arrived(wl_r.at[i], l_recv.at[i])
+        total += wl_r[i].astype(F32)
+    ws[...] = total
+    lax.fori_loop(1, 16, spread, 0)
+    pltpu.make_async_copy(piece(ws, sq), ws_r.at[0], s_recv.at[0]).start()
+
     def fold(i, acc):
         arrived(ws_r.at[i], s_recv.at[i])
         return acc + ws_r[i]
@@ -448,11 +462,15 @@
 
 
 def store(*refs):
-    sem = refs[-1]
-    copies = [pltpu.make_async_copy(refs[i], refs[6 + i], sem.at[i]) for i in range(6)]
-    for copy in copies:
+    ins, outs, held, sem = refs[:6], refs[6:12], refs[12:18], refs[18]
+    loads = [pltpu.make_async_copy(ins[i], held[i], sem.at[0, i]) for i in range(6)]
+    stores = [pltpu.make_async_copy(held[i], outs[i], sem.at[1, i]) for i in range(6)]
+    for copy in loads:
         copy.start()
-    for copy in copies:
+    for i in range(6):
+        loads[i].wait()
+        stores[i].start()
+    for copy in stores:
         copy.wait()
 
 
@@ -510,7 +528,7 @@
         out_shape=outs,
         in_specs=[hbm] * 6,
         out_specs=(hbm,) * 6,
-        scratch_shapes=[dma((6,))],
+        scratch_shapes=[buf(o.shape, o.dtype) for o in outs] + [dma((2, 6))],
         name="store",
         compiler_params=pltpu.CompilerParams(vmem_limit_bytes=VMEM),
     )(*results)

time: 108 us -> 86.3 us (0.80)
  the two profiles are of different devices: /device:TPU:113 before, /device:TPU:6 now
where the time goes in v3:
time: 86.3 us; the launch traced here: 86 us
  Pallas kernels  85.3 us (99%)
    pallas_call x1, Pallas kernels, body(): pl.pallas_call(kernel, out_shape=outs, in_specs=[hbm] * 9, out_specs=(hbm...  83.4 us
    pallas_call x1, Pallas kernels, body(): pl.pallas_call(store, out_shape=outs, in_specs=[hbm] * 6, out_specs=(hbm,...  1.94 us

profile of v3, /device:TPU:6, one launch (start us, length us, event | category | flops | bytes accessed | tf_op | source)
XLA Modules:
  0.0 86.0 jit_solution(5893958278616754681)
XLA Ops:
  0.6 83.4 %hstu.1 = (bf16[1,128,1024]{2,1,0:T(8,128)(2,1)}, bf16[1,128,512]{2,1,0:T(8,128)(2,1)}, bf16[1,128,512]{2,1,0:T(8,128)(2,1)}, bf16[1,128,512]{2,1,0:T(8,128)(2,1...) custom-call(bf16[1,128,512]{2,1,0:T(8,128)(2,1)} %q_ref.1, bf16[1,128,512]{2,1,0:T(8,128)(2,1)} %k_ref.1, ...), custom_call_target="tpu_custom_call" | custom-call | tf_op jit(solution)/shard_map/hstu/pallas_call | solution.py:515
  84.0 1.9 %store.1 = (bf16[1,128,1024]{2,1,0:T(8,128)(2,1)}, bf16[1,128,512]{2,1,0:T(8,128)(2,1)}, bf16[1,128,512]{2,1,0:T(8,128)(2,1)}, bf16[1,128,512]{2,1,0:T(8,128)(2,...) custom-call(bf16[1,128,1024]{2,1,0:T(8,128)(2,1)} %get-tuple-element.12.refs_0_, ...), custom_call_target="tpu_custom_call" | custom-call | tf_op jit(solution)/shard_map/store/pallas_call | solution.py:526

commit v4 on v3

--- a/solution.py
+++ b/solution.py
@@ -28,10 +28,10 @@
     lo_v, dq_v, dk_v, dv_v, gg_v, kv_s, q_s, g_v, w_v, len_v, own_v, pat_v,
     meta_s, meta_r, kv, rq, kt, wt, sl, low, high, att_t, att_s, ratt,
     dgat, gate_t, gated_t, gg_t, da_s, rda, dkv_f, sib_s, sib_r, dkv_s, rdkv, dq_t, dq_s, rdq,
-    dox, g_t, gx, wl_f, wl_s, wl_r, ws, ws_r, wa_s, wa,
+    dox, g_t, gx, wl_f, wl_s, wl_r, near, far_w, wa,
     in_sem, out_sem, kv_send, kv_recv, fwd_send, q_send, q_recv, meta_sem, att_send, att_recv,
     da_send, da_recv, sib_send, sib_recv, dkv_send, dkv_recv, dq_send, dq_recv,
-    do_send, do_recv, g_send, g_recv, l_send, l_recv, s_send, s_recv, a_send, a_recv,
+    do_send, do_recv, g_send, g_recv, l_send, l_recv, n_send, n_recv, f_send, f_recv,
 ):
     dp = lax.axis_index("dp")
     sq = lax.axis_index("seq")
@@ -89,8 +89,12 @@
     def l_dev(i):
         return (x * 8 + lax.rem(l + i, 4) * 2 + c, sq)
 
-    def s_dev(i):
-        return (dp, lax.rem(sq + i, 16))
+    def near_dev(i):
+        return (dp, (lax.div(y, 4) * 4 + lax.rem(y + i, 4)) * 2 + z)
+
+    def far_dev(i):
+        there = lax.rem(lax.div(y, 4) * 2 + z + i, 4)
+        return (dp, (lax.div(there, 2) * 4 + lax.rem(y, 4)) * 2 + lax.rem(there, 2))
 
     loads = []
 
@@ -126,8 +130,8 @@
         tell(x_dev(i, c))
         tell(x_dev(i, 1 - c))
         tell(l_dev(i))
-    for i in range(1, 16):
-        tell(s_dev(i))
+        tell(near_dev(i))
+        tell(far_dev(i))
 
     for copy in loads[:3]:
         copy.wait()
@@ -138,7 +142,7 @@
     for copy in loads[3:15]:
         copy.wait()
 
-    pl.semaphore_wait(barrier, 33 - jnp.where(own_par, 1, 0))
+    pl.semaphore_wait(barrier, 24 - jnp.where(own_par, 1, 0))
 
     meta_copy = remote(meta_s, meta_r, meta_sem.at[0], meta_sem.at[1], sib)
     meta_copy.start()
@@ -299,19 +303,6 @@
         core = c if cc == 0 else 1 - c
         remote(g_t.at[lax.rem(x + i, 4), core], gx.at[xc], g_send.at[n], g_recv.at[xc], to).start()
     gx[xc] = g_t[x, c]
-    lo_v[...] = dot(gated_t[...], w_v[...], TN).astype(BF16)
-    for h in range(H):
-        feats = slice(h * DH, (h + 1) * DH)
-        gg_v[:, feats] = gg_t[feats].T
-    outs = [
-        pltpu.make_async_copy(src, dst, out_sem.at[i])
-        for i, (src, dst) in enumerate((
-            (lo_v, lo_out.at[0]), (gg_v, gg_out.at[0]), (dq_v, dq_out.at[0]),
-            (dk_v, dk_out.at[0]), (dv_v, dv_out.at[0]), (wa, wg_out),
-        ))
-    ]
-    outs[0].start()
-    outs[1].start()
     for i in range(4):
         theirs = 2 * lax.rem(x + i, 4) + 1 - c
         arrived(dox.at[theirs], do_recv.at[theirs])
@@ -328,16 +319,6 @@
     for i in range(1, 4):
         there = lax.rem(l + i, 4)
         remote(wl_s.at[there], wl_r.at[i - 1], l_send.at[i - 1], l_recv.at[i - 1], l_dev(i)).start()
-
-    def piece(ref, s):
-        down = pl.multiple_of(lax.div(s, 8) * 8, 8)
-        across = pl.multiple_of(lax.rem(s, 8) * 128, 128)
-        return ref.at[pl.ds(down, 8), pl.ds(across, 128)]
-
-    def spread(i, _):
-        there = lax.rem(sq + i, 16)
-        remote(piece(ws, there), ws_r.at[i], s_send.at[i], s_recv.at[i], s_dev(i)).start()
-        return 0
 
     for k in range(4):
         arrived(rda.at[k], da_recv.at[k])
@@ -372,39 +353,57 @@
             dkv_s.at[i], rdkv.at[far, hh], dkv_send.at[i], dkv_recv.at[4 * far + hh], k, far == 1
         )
 
-    back(0)
-
     def back_step(i, _):
         back(i)
-        give(i - 1)
         return 0
 
-    lax.fori_loop(1, 8, back_step, 0)
-    for k in range(4):
-        dq_s[k] = dq_t[:, k * T : (k + 1) * T].T.astype(BF16)
-        push(dq_s.at[k], rdq.at[hh], dq_send.at[k], dq_recv.at[hh], k)
-    give(7)
+    def give_step(i, _):
+        give(i)
+        return 0
+
+    lax.fori_loop(0, 4, back_step, 0)
 
     total = wl_f[l]
     for i in range(3):
         arrived(wl_r.at[i], l_recv.at[i])
         total += wl_r[i].astype(F32)
-    ws[...] = total
-    lax.fori_loop(1, 16, spread, 0)
-    pltpu.make_async_copy(piece(ws, sq), ws_r.at[0], s_recv.at[0]).start()
-
-    def fold(i, acc):
-        arrived(ws_r.at[i], s_recv.at[i])
-        return acc + ws_r[i]
-
-    wa_s[...] = lax.fori_loop(0, 16, fold, jnp.zeros((8, 128), F32))
-
-    def share(i, _):
-        remote(wa_s, piece(wa, sq), a_send.at[i], a_recv.at[sq], s_dev(i)).start()
-        return 0
-
-    lax.fori_loop(1, 16, share, 0)
-    pltpu.make_async_copy(wa_s, piece(wa, sq), a_recv.at[sq]).start()
+    at_near = lax.rem(y, 4)
+    near[at_near] = total.astype(BF16)
+    for i in range(1, 4):
+        remote(near.at[at_near], near.at[at_near], n_send.at[i - 1], n_recv.at[at_near], near_dev(i)).start()
+
+    lax.fori_loop(0, 4, give_step, 0)
+    lax.fori_loop(4, 8, back_step, 0)
+
+    def gather_near():
+        for i in range(1, 4):
+            there = lax.rem(y + i, 4)
+            arrived(near.at[there], n_recv.at[there])
+        at_far = lax.div(y, 4) * 2 + z
+        total = sum(near[i].astype(F32) for i in range(4))
+        far_w[at_far] = total.astype(BF16)
+        for i in range(1, 4):
+            remote(far_w.at[at_far], far_w.at[at_far], f_send.at[i - 1], f_recv.at[at_far], far_dev(i)).start()
+
+    lax.fori_loop(4, 8, give_step, 0)
+    for k in range(4):
+        dq_s[k] = dq_t[:, k * T : (k + 1) * T].T.astype(BF16)
+        push(dq_s.at[k], rdq.at[hh], dq_send.at[k], dq_recv.at[hh], k)
+
+    gather_near()
+    lo_v[...] = dot(gated_t[...], w_v[...], TN).astype(BF16)
+    for h in range(H):
+        feats = slice(h * DH, (h + 1) * DH)
+        gg_v[:, feats] = gg_t[feats].T
+    outs = [
+        pltpu.make_async_copy(src, dst, out_sem.at[i])
+        for i, (src, dst) in enumerate((
+            (lo_v, lo_out.at[0]), (gg_v, gg_out.at[0]), (dq_v, dq_out.at[0]),
+            (dk_v, dk_out.at[0]), (dv_v, dv_out.at[0]), (wa, wg_out),
+        ))
+    ]
+    outs[0].start()
+    outs[1].start()
 
     for h in range(H):
         cols = slice(h * DH, (h + 1) * DH)
@@ -421,11 +420,10 @@
     outs[3].start()
     outs[4].start()
 
-    def gathered(i, _):
-        arrived(piece(wa, i), a_recv.at[i])
-        return 0
-
-    lax.fori_loop(0, 16, gathered, 0)
+    for i in range(1, 4):
+        there = lax.rem(lax.div(y, 4) * 2 + z + i, 4)
+        arrived(far_w.at[there], f_recv.at[there])
+    wa[...] = sum(far_w[i].astype(F32) for i in range(4))
     outs[5].start()
 
     for k in range(4):
@@ -450,13 +448,9 @@
         remote(gx.at[0], gx.at[0], g_send.at[i], g_recv.at[0], sib).wait_send()
     for i in range(3):
         remote(wl_s.at[0], wl_r.at[i], l_send.at[i], l_recv.at[i], sib).wait_send()
-
-    def left_seq(i, _):
-        remote(wa_s, ws_r.at[i], s_send.at[i], s_recv.at[i], sib).wait_send()
-        remote(wa_s, ws_r.at[i], a_send.at[i], a_recv.at[i], sib).wait_send()
-        return 0
-
-    lax.fori_loop(1, 16, left_seq, 0)
+        remote(near.at[0], near.at[0], n_send.at[i], n_recv.at[0], sib).wait_send()
+        remote(far_w.at[0], far_w.at[0], f_send.at[i], f_recv.at[0], sib).wait_send()
+
     for copy in outs:
         copy.wait()
 
@@ -502,15 +496,14 @@
         dq_t=buf((DH, 512), F32), dq_s=buf((4, T, DH), BF16), rdq=buf((4, T, DH), BF16),
         dox=buf((8, T, 1024), BF16), g_t=buf((4, 2, 4, 16, T), BF16), gx=buf((8, 4, 16, T), BF16),
         wl_f=buf((4, 16, 1024), F32), wl_s=buf((4, 16, 1024), BF16), wl_r=buf((3, 16, 1024), BF16),
-        ws=buf((16, 1024), F32), ws_r=buf((16, 8, 128), F32),
-        wa_s=buf((8, 128), F32), wa=buf((16, 1024), F32),
+        near=buf((4, 16, 1024), BF16), far_w=buf((4, 16, 1024), BF16), wa=buf((16, 1024), F32),
         in_sem=dma((18,)), out_sem=dma((6,)), kv_send=dma((8,)), kv_recv=dma((16,)), fwd_send=dma((8,)),
         q_send=dma((4,)), q_recv=dma((4,)), meta_sem=dma((2,)), att_send=dma((4,)), att_recv=dma((4,)),
         da_send=dma((4,)), da_recv=dma((4,)), sib_send=dma((8,)), sib_recv=dma((8,)),
         dkv_send=dma((8,)), dkv_recv=dma((8,)), dq_send=dma((4,)), dq_recv=dma((4,)),
         do_send=dma((7,)), do_recv=dma((8,)), g_send=dma((7,)), g_recv=dma((8,)),
         l_send=dma((3,)), l_recv=dma((3,)),
-        s_send=dma((16,)), s_recv=dma((16,)), a_send=dma((16,)), a_recv=dma((16,)),
+        n_send=dma((3,)), n_recv=dma((4,)), f_send=dma((3,)), f_recv=dma((4,)),
     )
     results = pl.pallas_call(
         kernel,

time: 86.3 us -> 80.9 us (0.937)
  the two profiles are of different devices: /device:TPU:6 before, /device:TPU:48 now
where the time goes in v4:
time: 80.9 us; the launch traced here: 80.7 us
  Pallas kernels  80.1 us (99%)
    pallas_call x1, Pallas kernels, body(): pl.pallas_call(kernel, out_shape=outs, in_specs=[hbm] * 9, out_specs=(hbm...  78.1 us
    pallas_call x1, Pallas kernels, body(): pl.pallas_call(store, out_shape=outs, in_specs=[hbm] * 6, out_specs=(hbm,...  1.94 us

profile of v4, /device:TPU:48, one launch (start us, length us, event | category | flops | bytes accessed | tf_op | source)
XLA Modules:
  0.0 80.7 jit_solution(3425585428853013270)
XLA Ops:
  0.6 78.1 %hstu.1 = (bf16[1,128,1024]{2,1,0:T(8,128)(2,1)}, bf16[1,128,512]{2,1,0:T(8,128)(2,1)}, bf16[1,128,512]{2,1,0:T(8,128)(2,1)}, bf16[1,128,512]{2,1,0:T(8,128)(2,1...) custom-call(bf16[1,128,512]{2,1,0:T(8,128)(2,1)} %q_ref.1, bf16[1,128,512]{2,1,0:T(8,128)(2,1)} %k_ref.1, ...), custom_call_target="tpu_custom_call" | custom-call | tf_op jit(solution)/shard_map/hstu/pallas_call | solution.py:508
  78.8 1.9 %store.1 = (bf16[1,128,1024]{2,1,0:T(8,128)(2,1)}, bf16[1,128,512]{2,1,0:T(8,128)(2,1)}, bf16[1,128,512]{2,1,0:T(8,128)(2,1)}, bf16[1,128,512]{2,1,0:T(8,128)(2,...) custom-call(bf16[1,128,1024]{2,1,0:T(8,128)(2,1)} %get-tuple-element.12.refs_0_, ...), custom_call_target="tpu_custom_call" | custom-call | tf_op jit(solution)/shard_map/store/pallas_call | solution.py:519

commit v5 on v4

--- a/solution.py
+++ b/solution.py
@@ -309,11 +309,10 @@
         arrived(gx.at[theirs], g_recv.at[theirs])
         if i:
             arrived(gx.at[theirs + 2 * c - 1], g_recv.at[theirs + 2 * c - 1])
+    side = jnp.concatenate([gx[i].reshape(64, T) for i in range(8)], axis=1)
     for n in range(2):
         cols = slice(n * 512, (n + 1) * 512)
-        part = dot(gx[0].reshape(64, T), dox[0, :, cols])
-        for i in range(1, 8):
-            part += dot(gx[i].reshape(64, T), dox[i, :, cols])
+        part = dot(side, dox[:, :, cols].reshape(1024, 512))
         wl_f[:, :, cols] = part.reshape(4, 16, 512)
         wl_s[:, :, cols] = part.astype(BF16).reshape(4, 16, 512)
     for i in range(1, 4):
@@ -374,7 +373,6 @@
 
     lax.fori_loop(0, 4, give_step, 0)
     lax.fori_loop(4, 8, back_step, 0)
-
     def gather_near():
         for i in range(1, 4):
             there = lax.rem(y + i, 4)

time: 80.9 us -> 80.9 us (level)
  no operation moved by 1% of the time
where the time goes in v5:
time: 80.9 us; the launch traced here: 80.8 us
  Pallas kernels  80.1 us (99%)
    pallas_call x1, Pallas kernels, body(): pl.pallas_call(kernel, out_shape=outs, in_specs=[hbm] * 9, out_specs=(hbm...  78.2 us
    pallas_call x1, Pallas kernels, body(): pl.pallas_call(store, out_shape=outs, in_specs=[hbm] * 6, out_specs=(hbm,...  1.94 us

profile of v5, /device:TPU:48, one launch (start us, length us, event | category | flops | bytes accessed | tf_op | source)
XLA Modules:
  0.0 80.8 jit_solution(8037962138003518420)
XLA Ops:
  0.6 78.2 %hstu.1 = (bf16[1,128,1024]{2,1,0:T(8,128)(2,1)}, bf16[1,128,512]{2,1,0:T(8,128)(2,1)}, bf16[1,128,512]{2,1,0:T(8,128)(2,1)}, bf16[1,128,512]{2,1,0:T(8,128)(2,1...) custom-call(bf16[1,128,512]{2,1,0:T(8,128)(2,1)} %q_ref.1, bf16[1,128,512]{2,1,0:T(8,128)(2,1)} %k_ref.1, ...), custom_call_target="tpu_custom_call" | custom-call | tf_op jit(solution)/shard_map/hstu/pallas_call | solution.py:506
  78.8 1.9 %store.1 = (bf16[1,128,1024]{2,1,0:T(8,128)(2,1)}, bf16[1,128,512]{2,1,0:T(8,128)(2,1)}, bf16[1,128,512]{2,1,0:T(8,128)(2,1)}, bf16[1,128,512]{2,1,0:T(8,128)(2,...) custom-call(bf16[1,128,1024]{2,1,0:T(8,128)(2,1)} %get-tuple-element.12.refs_0_, ...), custom_call_target="tpu_custom_call" | custom-call | tf_op jit(solution)/shard_map/store/pallas_call | solution.py:517
